TPU v7x, 1024 devices: a whole 8x8x8 slice. The times are simulated.
1024 devices in a mesh: ctx: 16 (over x, z_hi), exp: 64 (over y, z_lo, core).
Axes of the slice: x: 8, y: 8, z: 8 (z_hi: 2, z_lo: 4; z = z_hi * 4 + z_lo), core: 2. Of those that a mesh axis runs over, the one named last changes fastest.
Arguments:
- hidden_in: bfloat16 [1024, 4096], P('ctx'), may hold values from -0.59765625 to 0.59765625
- queries: bfloat16 [1024, 8192], P('ctx', 'exp'), may hold values from -120 to 120
- keys: bfloat16 [1024, 512], P('ctx'), may hold values from -6 to 6
- values: bfloat16 [1024, 512], P('ctx'), may hold values from -6 to 6
- out_proj: bfloat16 [8192, 4096], P('exp'), may hold values from -0.0625 to 0.0625
- norm_gain: float32 [4096], replicated, may hold values from 0.5 to 1.5
- routes: int32 [1024, 8], P('ctx'), may hold values from 0 to 63, all different within a row; in each aligned block of 64 rows (0 to 63, 64 to 127, ...) at most 16 rows name the same one
- gates: float32 [1024, 8], P('ctx'), may hold values from 0.05 to 0.3
- w_gate: bfloat16 [64, 4096, 1536], P('exp', None, 'ctx'), may hold values from -0.09375 to 0.09375
- w_up: bfloat16 [64, 4096, 1536], P('exp', None, 'ctx'), may hold values from -0.09375 to 0.09375
- w_down: bfloat16 [64, 1536, 4096], P('exp', 'ctx'), may hold values from -0.15625 to 0.15625
Outputs:
- layer_out: bfloat16 [1024, 4096], P(('ctx', 'exp'))
Inputs may be any that keep to these rules, and one draw needn't show every extreme that they name: `routes`: each row names 8 distinct experts. Within each sequence shard's 64 rows no expert is named by more than 16 rows, a bound that some block reaches.
All inputs are finite; a program needn't handle non-finite values.
Results may differ from a plain program's by a relative error of at most 0.02.
Values may be sent and summed in bfloat16 or wider, within the bound.
A program may use at most 32 MiB of HBM per device.

v0:
```python
import jax
import jax.numpy as jnp
from jax import lax
from jax.sharding import PartitionSpec as P

HEADS = 64
KVH = 4
HD = 128
TOP = 8


highest = lax.Precision.HIGHEST


def rms_norm(rows_in, norm_gain):
    mean_square = jnp.mean(rows_in * rows_in, axis=1, keepdims=True)
    return (rows_in * lax.rsqrt(mean_square + 1e-06) * norm_gain).astype(jnp.bfloat16)


def local(
    hidden_in, queries, keys, values, out_proj, norm_gain, routes, gates, w_gate, w_up, w_down
):
    tok_rows = queries.shape[0]
    head_count = queries.shape[1] // HD
    group_size = HEADS // KVH
    head_first = lax.axis_index("exp") * head_count
    kv_start = head_first // group_size * HD
    own_keys = lax.dynamic_slice_in_dim(keys, kv_start, HD, 1)
    own_values = lax.dynamic_slice_in_dim(values, kv_start, HD, 1)
    query_pos = lax.axis_index("ctx") * tok_rows + jnp.arange(tok_rows, dtype=jnp.int32)
    query_flat = (
        queries.reshape(tok_rows, head_count, HD)
        .transpose(1, 0, 2)
        .reshape(head_count * tok_rows, HD)
    )
    row_pos = jnp.tile(query_pos, head_count)
    score_scale = HD ** (-0.5)
    flat_rows = head_count * tok_rows
    running_max = jnp.full((flat_rows,), -1e30, jnp.float32)
    key_piece = lax.all_gather(own_keys, "ctx", axis=0, tiled=True)
    value_piece = lax.all_gather(own_values, "ctx", axis=0, tiled=True)
    key_count = key_piece.shape[0]
    scores = (
        lax.dot_general(
            query_flat, key_piece, (((1,), (1,)), ((), ())), preferred_element_type=jnp.float32
        )
        * score_scale
    )
    key_pos = jnp.arange(key_count, dtype=jnp.int32)
    visible = key_pos[None, :] <= row_pos[:, None]
    masked = jnp.where(visible, scores, -1e30)
    new_max = jnp.maximum(running_max, jnp.max(masked, axis=1))
    prob_raw = jnp.where(visible, jnp.exp(masked - new_max[:, None]), 0.0)
    running_sum = jnp.sum(prob_raw, axis=1)
    numerator = jnp.dot(
        prob_raw.astype(jnp.bfloat16), value_piece, preferred_element_type=jnp.float32
    )
    attended = (numerator / running_sum[:, None]).astype(jnp.bfloat16)
    attended = (
        attended.reshape(head_count, tok_rows, HD)
        .transpose(1, 0, 2)
        .reshape(tok_rows, head_count * HD)
    )
    exp_size = lax.axis_size("exp")
    row_share = tok_rows // exp_size
    row_first = lax.axis_index("exp") * row_share
    attn_sum = lax.psum(jnp.dot(attended, out_proj, preferred_element_type=jnp.float32), "exp")
    mixed_all = hidden_in.astype(jnp.float32) + attn_sum
    normed = rms_norm(mixed_all, norm_gain)
    mixed_rows = lax.dynamic_slice_in_dim(mixed_all, row_first, row_share, 0)
    slot_count = min(tok_rows, 2 * tok_rows * TOP // exp_size)
    expert_id = lax.axis_index("exp")
    route_hit = routes == expert_id
    token_weight = jnp.sum(jnp.where(route_hit, gates, 0.0), axis=1)
    member = jnp.any(route_hit, axis=1)
    slot_index = jnp.cumsum(member.astype(jnp.int32)) - 1
    slot_ids = jnp.arange(slot_count, dtype=jnp.int32)
    select = ((slot_index[None, :] == slot_ids[:, None]) & member[None, :]).astype(jnp.float32)
    picked = jnp.dot(
        select.astype(jnp.bfloat16), normed, preferred_element_type=jnp.float32
    ).astype(jnp.bfloat16)
    slot_weight = jnp.dot(select, token_weight, precision=highest)
    block_rows = lax.all_gather(picked, "ctx", axis=0, tiled=True)
    gate_val = jnp.dot(block_rows, w_gate[0], preferred_element_type=jnp.float32)
    up_val = jnp.dot(block_rows, w_up[0], preferred_element_type=jnp.float32)
    act = (jax.nn.silu(gate_val) * up_val).astype(jnp.bfloat16)
    partials = jnp.dot(act, w_down[0], preferred_element_type=jnp.float32)
    expert_out = lax.psum_scatter(
        partials.astype(jnp.bfloat16), "ctx", scatter_dimension=0, tiled=True
    ).astype(jnp.float32)
    scaled = slot_weight[:, None] * expert_out
    select_t = select.T
    moe_rows = lax.psum_scatter(
        jnp.dot(select_t, scaled, precision=highest, preferred_element_type=jnp.float32),
        "exp",
        scatter_dimension=0,
        tiled=True,
    )
    return (mixed_rows + moe_rows).astype(jnp.bfloat16)


def solution(mesh):
    return jax.shard_map(
        local,
        mesh=mesh,
        in_specs=(
            P("ctx", None),
            P("ctx", "exp"),
            P("ctx", None),
            P("ctx", None),
            P("exp", None),
            P(),
            P("ctx", None),
            P("ctx", None),
            P("exp", None, "ctx"),
            P("exp", None, "ctx"),
            P("exp", "ctx", None),
        ),
        out_specs=P(("ctx", "exp"), None),
        check_vma=False,
    )
```

profile of v0, /device:TPU:1, one launch (start us, length us, event | category | flops | bytes accessed | tf_op | source)
XLA Modules:
  0.0 1579.3 jit_solution(10833701382040296696)
XLA Ops:
  6.5 0.0 copy-start
  6.5 0.0 all-reduce.4.cloned.1.call-start
  6.5 0.8 constant_dynamic-slice_fusion.1
  7.4 0.7 constant_dynamic-slice_fusion
  8.1 55.5 %all_gather.10 = bf16[1024,128]{1,0:T(8,128)(2,1)S(1)} all-gather(bf16[64,128]{1,0:T(8,128)(2,1)S(1)} %constant_dynamic-slice_fusion), channel_id=1, replica_groups=mesh['ctx'=16,'exp'=64] {'ctx'}, dimensions={0}, use_global_device_ids=true | all-gather | bytes 278528 | tf_op jit(solution)/shard_map/all_gather | solution.py:41
  63.6 39.8 %all_gather.9 = bf16[1024,128]{1,0:T(8,128)(2,1)S(1)} all-gather(bf16[64,128]{1,0:T(8,128)(2,1)S(1)} %constant_dynamic-slice_fusion.1), channel_id=1, replica_groups=mesh['ctx'=16,'exp'=64] {'ctx'}, dimensions={0}, use_global_device_ids=true | all-gather | bytes 278528 | tf_op jit(solution)/shard_map/all_gather | solution.py:40
  103.4 1.0 fusion.47
  104.4 0.0 copy-start.5
  104.4 0.0 copy-start.6
  104.4 0.0 copy-start.3
  104.4 0.2 fusion.15
  104.7 0.0 copy-done
  104.7 1.5 fusion.4
  106.2 0.0 copy-start.4
  106.2 0.0 all-reduce.4.cloned.1.call-update
  106.2 0.0 all-gather.2.cloned.1.call-start
  106.3 0.0 copy-done.5
  106.3 0.0 copy-done.6
  106.4 0.1 copy.14
  106.5 0.1 reduce-window.8
  106.5 0.1 add_reduce_fusion
  106.7 563.0 %all-reduce.4.cloned.1.call-done = f32[64,4096]{1,0:T(8,128)} async-done(((f32[64,4096]{1,0:T(8,128)}), f32[64,4096]{1,0:T(8,128)}) %all-reduce.4.cloned.1.call-update) | async-done | bytes 1048592 | tf_op jit(solution)/shard_map/psum | solution.py:67
  669.7 0.0 copy-done.3
  669.7 1.5 multiply_reduce_fusion
  671.1 0.0 copy-start.2
  671.2 1.0 copy-done.2
  672.1 0.0 copy-done.4
  672.1 0.9 convolution_convert_fusion.1
  673.1 0.0 all-gather.2.cloned.1.call-update
  673.1 0.0 reduce-scatter.2.cloned.1.call-start
  673.1 111.6 %all-gather.2.cloned.1.call-done = bf16[256,4096]{1,0:T(8,128)(2,1)} async-done(((bf16[16,4096]{1,0:T(8,128)(2,1)}), bf16[256,4096]{1,0:T(8,128)(2,1)}) %all-gather.2.cloned.1.call-update) | async-done | bytes 2097168 | tf_op jit(solution)/shard_map/all_gather | solution.py:83
  784.7 0.0 copy-start.1
  784.7 2.7 fusion.8
  787.4 0.0 copy-done.1
  787.4 5.3 convolution_convert_fusion
  792.7 0.0 reduce-scatter.2.cloned.1.call-update
  792.7 0.0 all-reduce.6.cloned.1.call-start
  792.7 0.1 convolution_bitcast_fusion
  792.9 228.1 %reduce-scatter.2.cloned.1.call-done = bf16[16,4096]{1,0:T(8,128)(2,1)} async-done(((bf16[256,4096]{1,0:T(8,128)(2,1)}), bf16[16,4096]{1,0:T(8,128)(2,1)}) %reduce-scatter.2.cloned.1.call-update) | async-done | bytes 131088 | tf_op jit(solution)/shard_map/reduce_scatter | solution.py:88
  1021.0 2.6 fusion.12
  1023.6 0.0 all-reduce.6.cloned.1.call-update
  1023.6 1.2 dynamic-slice
  1024.8 545.8 %all-reduce.6.cloned.1.call-done = f32[64,4096]{1,0:T(8,128)} async-done(((f32[64,4096]{1,0:T(8,128)}), f32[64,4096]{1,0:T(8,128)}) %all-reduce.6.cloned.1.call-update) | async-done | bytes 1048592
  1570.7 2.1 fusion.32
  (6 shorter events, 0.1 us)
Async XLA Ops:
  6.5 98.1 %copy-start = (bf16[128,4096]{1,0:T(8,128)(2,1)S(1)}, bf16[128,4096]{1,0:T(8,128)(2,1)}, u32[]{:S(2)}) copy-start(bf16[128,4096]{1,0:T(8,128)(2,1)} %param.15) | copy-start | bytes 3145732
  6.5 663.1 %all-reduce.4.cloned.1.call-start = ((), (), s32[]{:S(2)}) async-start(), calls=%async_computation.1 | async-start | bytes 2097152 | tf_op jit(solution)/shard_map/psum | solution.py:67
  104.4 1.9 copy-start.5
  104.4 1.9 copy-start.6
  104.4 565.3 %copy-start.3 = (bf16[64,4096]{1,0:T(8,128)(2,1)S(1)}, bf16[64,4096]{1,0:T(8,128)(2,1)}, u32[]{:S(2)}) copy-start(bf16[64,4096]{1,0:T(8,128)(2,1)} %param.11) | copy-start | bytes 1572868
  106.2 565.9 %copy-start.4 = (f32[4096]{0:T(1024)S(1)}, f32[4096]{0:T(1024)}, u32[]{:S(2)}) copy-start(f32[4096]{0:T(1024)} %param.16) | copy-start | bytes 49156
  106.2 678.5 %all-gather.2.cloned.1.call-start = ((), (), s32[]{:S(2)}) async-start(), calls=%async_computation.2 | async-start | bytes 2228224 | tf_op jit(solution)/shard_map/all_gather | solution.py:83
  671.1 1.0 copy-start.2
  673.1 347.9 %reduce-scatter.2.cloned.1.call-start = ((), (), s32[]{:S(2)}) async-start(), calls=%async_computation.3 | async-start | bytes 2228224 | tf_op jit(solution)/shard_map/reduce_scatter | solution.py:88
  784.7 2.7 copy-start.1
  792.7 778.0 %all-reduce.6.cloned.1.call-start = ((), (), s32[]{:S(2)}) async-start(), calls=%async_computation.4 | async-start | bytes 2097152
Sparse Core Ops, SparseCore 0:
  106.4 563.2 all-reduce.3
  674.8 109.8 all-gather.1
  792.8 228.1 reduce-scatter.1
  1024.3 546.2 all-reduce.5
where the time goes:
time: 1580 us
  waiting for transfers between devices  1450 us (92%)
  blocking collectives  95.3 us (6%)
    psum x1, waiting for transfers between devices, local(): lax.psum(jnp.dot(attended, out_proj, preferred_element_type=jnp.float32),...  563 us
    unnamed x5, waiting for transfers between devices  546 us
    reduce_scatter x1, waiting for transfers between devices, local(): lax.psum_scatter(partials.astype(jnp.bfloat16), 'ctx', scatter_dimension=...  228 us
    all_gather x1, waiting for transfers between devices, local(): block_rows = lax.all_gather(picked, 'ctx', axis=0, tiled=True)  112 us
    all_gather x1, blocking collectives, local(): value_piece = lax.all_gather(own_values, 'ctx', axis=0, tiled=True)  55.5 us
    all_gather x1, blocking collectives, local(): key_piece = lax.all_gather(own_keys, 'ctx', axis=0, tiled=True)  39.8 us
  transfers between devices with their start and end apart: 4, of which 4 were waited for; matrix products, arithmetic and copies ran while one was open for 0% of the time, Pallas kernels for 0%

commit v1 on v0

v1 whole, which is shorter than its diff:
```python
import functools

import jax
import jax.numpy as jnp
from jax import lax
from jax.experimental import pallas as pl
from jax.experimental.pallas import tpu as pltpu
from jax.sharding import PartitionSpec as P

HEADS = 64
KVH = 4
SLOTS = 16
ZH, ZL, CO = 2, 4, 2
MESH = pl.DeviceIdType.MESH
F32, BF16 = jnp.float32, jnp.bfloat16
NT = (((1,), (1,)), ((), ()))
TN = (((0,), (0,)), ((), ()))


def kernel(
    nctx, nexp,
    hidden_in, queries, keys, values, out_proj, norm_gain, routes, gates, w_gate, w_up, w_down,
    out_ref,
    kv, qv, hid, wo, gain, rt, gt, wg, wu,
    pbuf, crecv, acc, rsy, acc2, rsz, ag,
    mt, wd, rows, act, act_t, oacc, expand, gated, r5c, acc5, r5y, acc6, r5z, snd, fin, own,
    lsem,
    s_kv, r_kv, s_kvc, r_kvc, s_sel, r_sel, s_wd, r_wd,
    s_c, r_c, s_y, r_y, s_z, r_z, s_gz, r_gz, s_gy, r_gy, s_gc, r_gc,
    s_zh, r_zh, s_ring, r_ring, s_azh, r_azh, s_aring, r_aring,
    s_5c, r_5c, s_5y, r_5y, s_5z, r_5z, s_f, r_f,
):
    nx, ny = nctx // ZH, nexp // (ZL * CO)
    tok, hd = qv.shape
    dim = hid.shape[1]
    ffs = w_down.shape[1]
    half = tok // 2
    dy, dz = dim // ny, dim // ny // ZL
    dc = dim // nctx
    c, e = lax.axis_index("ctx"), lax.axis_index("exp")
    x, zh = lax.div(c, ZH), lax.rem(c, ZH)
    y, zl, co = lax.div(e, ZL * CO), lax.rem(lax.div(e, CO), ZL), lax.rem(e, CO)
    core_e = e + 1 - 2 * co
    oco = 1 - co

    def ctx_at(xx, hh):
        return lax.rem(xx + nx, nx) * ZH + hh

    def exp_at(yy, zz, cc):
        return (yy * ZL + zz) * CO + cc

    sent = []

    def put(src, dst, ssem, rsem, cc, ee):
        copy = pltpu.make_async_remote_copy(
            src_ref=src, dst_ref=dst, send_sem=ssem, recv_sem=rsem,
            device_id=(cc, ee), device_id_type=MESH,
        )
        copy.start()
        sent.append(copy)
        return copy

    def landed(ref, rsem):
        pltpu.make_async_remote_copy(
            src_ref=ref, dst_ref=ref, send_sem=rsem, recv_sem=rsem,
            device_id=(c, core_e), device_id_type=MESH,
        ).wait_recv()

    def al(v, m):
        return pl.multiple_of(v, m)

    group = HEADS // KVH
    heads_here = max(1, HEADS // nexp)
    kv_col = al(lax.div(e * heads_here, group) * hd, hd)
    own_kv = kv.at[co, pl.ds(al(c * tok, tok), tok)]

    @pl.when(co == 0)
    def _():
        pltpu.make_async_copy(keys.at[:, pl.ds(kv_col, hd)], own_kv, lsem.at[0]).start()

    @pl.when(co == 1)
    def _():
        pltpu.make_async_copy(values.at[:, pl.ds(kv_col, hd)], own_kv, lsem.at[0]).start()

    own_wd = pltpu.make_async_copy(
        w_down.at[0, :, pl.ds(al(c * dc, dc), dc)], wd.at[pl.ds(al(c * ffs, ffs), ffs)], lsem.at[1]
    )
    loads = [
        pltpu.make_async_copy(src, dst, lsem.at[2 + i])
        for i, (src, dst) in enumerate([
            (routes, rt), (gates, gt), (queries, qv), (out_proj, wo), (hidden_in, hid),
            (norm_gain, gain), (w_gate.at[0], wg), (w_up.at[0], wu),
        ])
    ]
    for load in loads:
        load.start()
    own_wd.start()

    barrier = pltpu.get_barrier_semaphore()

    def greet(cc, ee):
        pl.semaphore_signal(barrier, inc=1, device_id=(cc, ee), device_id_type=MESH)

    for d in range(1, nctx):
        greet(lax.rem(c + d, nctx), e)
    for d in range(1, ny):
        greet(c, exp_at(lax.rem(y + d, ny), zl, co))
    for d in range(1, ZL):
        greet(c, exp_at(y, lax.rem(zl + d, ZL), co))
    greet(c, core_e)
    pl.semaphore_wait(barrier, (nctx - 1) + (ny - 1) + (ZL - 1) + 1)

    pltpu.make_async_copy(keys.at[:, pl.ds(kv_col, hd)], own_kv, lsem.at[0]).wait()
    for d in range(1, nctx):
        put(own_kv, own_kv, s_kv.at[d - 1], r_kv.at[d - 1], lax.rem(c + d, nctx), e)

    loads[0].wait()
    loads[1].wait()
    hit = rt[...] == e
    member = jnp.max(jnp.where(hit, 1.0, 0.0), axis=1, keepdims=True)
    weight = jnp.sum(jnp.where(hit, gt[...], 0.0), axis=1, keepdims=True)
    wide = mt.shape[1]
    t_row = lax.broadcasted_iota(jnp.int32, (tok, wide), 0)
    t_col = lax.broadcasted_iota(jnp.int32, (tok, wide), 1)
    same = jnp.where(t_row == t_col, 1.0, 0.0)
    upto = jnp.where(t_row <= t_col, 1.0, 0.0)
    member_r = jnp.sum(member * same, axis=0, keepdims=True)
    weight_r = jnp.sum(weight * same, axis=0, keepdims=True)
    count_r = jnp.sum(member * upto, axis=0, keepdims=True)
    slot_i = lax.broadcasted_iota(jnp.int32, (SLOTS, wide), 0).astype(F32)
    chosen = (count_r - 1.0 == slot_i) & (member_r > 0.0)
    own_mt = mt.at[pl.ds(al(c * SLOTS, SLOTS), SLOTS)]
    own_mt[...] = jnp.where(chosen, weight_r, 0.0)
    pick = jnp.where(chosen, 1.0, 0.0)
    mine = jnp.where(lax.broadcasted_iota(jnp.int32, (SLOTS, wide), 1) == e, 1.0, 0.0)
    pick2 = jnp.concatenate([pick, mine], axis=0)[:, :tok].astype(BF16)

    for d in range(1, nctx):
        src = lax.rem(c + nctx - d, nctx)
        landed(kv.at[co, pl.ds(al(src * tok, tok), tok)], r_kv.at[d - 1])
    put(kv.at[co], kv.at[co], s_kvc, r_kvc, c, core_e)
    for d in range(1, nctx):
        put(own_mt, own_mt, s_sel.at[d - 1], r_sel.at[d - 1], lax.rem(c + d, nctx), e)
    loads[2].wait()
    landed(kv.at[oco], r_kvc)

    scores = lax.dot_general(qv[...], kv[0], NT, preferred_element_type=F32) * hd ** (-0.5)
    n_keys = kv.shape[1]
    q_pos = c * tok + lax.broadcasted_iota(jnp.int32, (tok, n_keys), 0)
    visible = lax.broadcasted_iota(jnp.int32, (tok, n_keys), 1) <= q_pos
    masked = jnp.where(visible, scores, -1e30)
    prob = jnp.where(visible, jnp.exp(masked - jnp.max(masked, axis=1, keepdims=True)), 0.0)
    total = jnp.sum(prob, axis=1, keepdims=True)
    numer = jnp.dot(prob.astype(BF16), kv[1], preferred_element_type=F32)
    att = (numer / total).astype(BF16)
    loads[3].wait()
    for j in range(ny):
        cols = pl.ds(j * dy, dy)
        pbuf[:, cols] = jnp.dot(att, wo[:, cols], preferred_element_type=F32).astype(BF16)

    put(pbuf.at[pl.ds(al(oco * half, half), half)], crecv, s_c, r_c, c, core_e)
    for d in range(1, nctx):
        t = lax.rem(c + d, nctx)
        put(
            w_down.at[0, :, pl.ds(al(t * dc, dc), dc)], wd.at[pl.ds(al(c * ffs, ffs), ffs)],
            s_wd.at[d - 1], r_wd.at[d - 1], t, e,
        )
    landed(crecv, r_c)
    mine_rows = pl.ds(al(co * half, half), half)
    for j in range(ny):
        cols = pl.ds(j * dy, dy)
        acc[:, cols] = (pbuf[mine_rows, cols].astype(F32) + crecv[:, cols].astype(F32)).astype(BF16)
    for d in range(1, ny):
        t = lax.rem(y + d, ny)
        put(acc.at[:, pl.ds(al(t * dy, dy), dy)], rsy.at[d - 1], s_y.at[d - 1], r_y.at[d - 1], c, exp_at(t, zl, co))
    tot = acc[:, pl.ds(al(y * dy, dy), dy)].astype(F32)
    for d in range(1, ny):
        landed(rsy.at[d - 1], r_y.at[d - 1])
        tot = tot + rsy[d - 1].astype(F32)
    acc2[...] = tot.astype(BF16)
    for d in range(1, ZL):
        t = lax.rem(zl + d, ZL)
        put(acc2.at[:, pl.ds(al(t * dz, dz), dz)], rsz.at[d - 1], s_z.at[d - 1], r_z.at[d - 1], c, exp_at(y, t, co))
    tot = acc2[:, pl.ds(al(zl * dz, dz), dz)].astype(F32)
    for d in range(1, ZL):
        landed(rsz.at[d - 1], r_z.at[d - 1])
        tot = tot + rsz[d - 1].astype(F32)
    piece = pl.ds(al(y * dy + zl * dz, dz), dz)
    ag[mine_rows, piece] = tot.astype(BF16)
    for d in range(1, ZL):
        put(ag.at[mine_rows, piece], ag.at[mine_rows, piece], s_gz.at[d - 1], r_gz.at[d - 1], c, exp_at(y, lax.rem(zl + d, ZL), co))
    for d in range(1, ZL):
        src = lax.rem(zl + ZL - d, ZL)
        landed(ag.at[mine_rows, pl.ds(al(y * dy + src * dz, dz), dz)], r_gz.at[d - 1])
    piece = pl.ds(al(y * dy, dy), dy)
    for d in range(1, ny):
        put(ag.at[mine_rows, piece], ag.at[mine_rows, piece], s_gy.at[d - 1], r_gy.at[d - 1], c, exp_at(lax.rem(y + d, ny), zl, co))
    for d in range(1, ny):
        src = lax.rem(y + ny - d, ny)
        landed(ag.at[mine_rows, pl.ds(al(src * dy, dy), dy)], r_gy.at[d - 1])
    put(ag.at[mine_rows], ag.at[mine_rows], s_gc, r_gc, c, core_e)
    loads[4].wait()
    loads[5].wait()
    landed(ag.at[pl.ds(al(oco * half, half), half)], r_gc)

    square = jnp.zeros((SLOTS, 1), F32)
    mixes = []
    for j in range(ny):
        cols = pl.ds(j * dy, dy)
        mixed = jnp.dot(pick2, ag[:, cols], preferred_element_type=F32) + jnp.dot(
            pick2, hid[:, cols], preferred_element_type=F32
        )
        square = square + jnp.sum(mixed[:SLOTS] * mixed[:SLOTS], axis=1, keepdims=True)
        for k in range(dy // dc):
            own[j * (dy // dc) + k] = mixed[SLOTS : SLOTS + 1, k * dc : (k + 1) * dc]
        mixes.append(mixed[:SLOTS])
    scale = lax.rsqrt(square / dim + 1e-06)
    for j in range(ny):
        cols = pl.ds(j * dy, dy)
        rows[c, :, cols] = (mixes[j] * scale * gain[:, cols]).astype(BF16)

    hops = {(1, 0): nx // 2, (-1, 0): nx // 2 - 1, (1, 1): nx // 2 - 1, (-1, 1): nx // 2}
    first = {}
    n = 0
    for key in hops:
        first[key] = n
        n += hops[key]

    def ring(at, s_zh, r_zh, s_ring, r_ring, use):
        side = (zh, 1 - zh)

        def send(key, k):
            step, kind = key
            if k < hops[key]:
                ref = at(ctx_at(x - step * k, side[kind]))
                i = first[key] + k
                put(ref, ref, s_ring.at[i], r_ring.at[i], ctx_at(x + step, zh), e)

        def wait(key, k):
            step, kind = key
            block = ctx_at(x - step * k, side[kind])
            landed(at(block), r_ring.at[first[key] + k - 1])
            return block

        put(at(c), at(c), s_zh, r_zh, ctx_at(x, 1 - zh), e)
        send((1, 0), 0)
        send((-1, 0), 0)
        held = [c]
        for k in range(1, nx // 2 + 2):
            arrived = []
            for step in (1, -1):
                if k <= hops[(step, 0)]:
                    arrived.append(wait((step, 0), k))
                    send((step, 0), k)
            for step in (1, -1):
                if k == 1:
                    if step == 1:
                        partner = ctx_at(x, 1 - zh)
                        landed(at(partner), r_zh)
                        held.append(partner)
                    send((step, 1), 0)
                elif k - 1 <= hops[(step, 1)]:
                    held.append(wait((step, 1), k - 1))
                    send((step, 1), k - 1)
            use(held)
            held = arrived
        if held:
            use(held)

    for load in loads[6:]:
        load.wait()
    kc = dim // 4

    def expert(blocks):
        g = jnp.zeros((len(blocks) * SLOTS, ffs), F32)
        u = jnp.zeros((len(blocks) * SLOTS, ffs), F32)
        for k in range(4):
            part = pl.ds(k * kc, kc)
            rows_in = jnp.concatenate([rows[b, :, part] for b in blocks], axis=0)
            g = g + jnp.dot(rows_in, wg[part], preferred_element_type=F32)
            u = u + jnp.dot(rows_in, wu[part], preferred_element_type=F32)
        a = g / (1.0 + jnp.exp(-g)) * u
        for i, b in enumerate(blocks):
            act[pl.ds(al(b * SLOTS, SLOTS), SLOTS), :ffs] = a[i * SLOTS : (i + 1) * SLOTS]

    ring(lambda b: rows.at[b], s_zh, r_zh, s_ring, r_ring, expert)
    act_t[pl.ds(al(c * ffs, ffs), ffs), :] = act[...].T[:ffs].astype(BF16)

    for d in range(1, nctx):
        landed(mt.at[pl.ds(al(lax.rem(c + nctx - d, nctx) * SLOTS, SLOTS), SLOTS)], r_sel.at[d - 1])
    n_out = tok * nctx

    def place(i, _):
        blk = n_out // 8
        r = i * blk + lax.broadcasted_iota(jnp.int32, (blk, wide), 0)
        t = lax.broadcasted_iota(jnp.int32, (blk, wide), 1)
        p = lax.div(r, nctx)
        token = lax.rem(p, tok // CO) * CO + lax.div(p, tok // CO)
        pattern = jnp.where(t == token, 1.0, 0.0).astype(BF16)
        taken = jnp.where(mt[...] > 0.0, 1.0, 0.0).astype(BF16)
        hits = lax.dot_general(pattern, taken, NT, preferred_element_type=F32)
        r = i * blk + lax.broadcasted_iota(jnp.int32, hits.shape, 0)
        s = lax.broadcasted_iota(jnp.int32, hits.shape, 1)
        keep = lax.rem(r, nctx) == lax.div(s, SLOTS)
        expand[pl.ds(al(i * blk, blk), blk), :] = jnp.where(keep, hits, 0.0).astype(BF16)
        return 0

    lax.fori_loop(0, 8, place, 0)
    oacc[...] = jnp.zeros_like(oacc)
    own_wd.wait()
    for d in range(1, nctx):
        landed(wd.at[pl.ds(al(lax.rem(c + nctx - d, nctx) * ffs, ffs), ffs)], r_wd.at[d - 1])

    def down(blocks):
        tot = oacc[...]
        for b in blocks:
            part = pl.ds(al(b * ffs, ffs), ffs)
            tot = tot + lax.dot_general(act_t[part], wd[part], TN, preferred_element_type=F32)
        oacc[...] = tot

    ring(lambda b: act_t.at[pl.ds(al(b * ffs, ffs), ffs)], s_azh, r_azh, s_aring, r_aring, down)

    scaled = (oacc[...] * jnp.sum(mt[...], axis=1, keepdims=True)).astype(BF16)
    h5 = n_out // 2
    theirs = pl.ds(al(oco * h5, h5), h5)
    ours = pl.ds(al(co * h5, h5), h5)
    gated[theirs] = jnp.dot(expand[theirs], scaled, preferred_element_type=F32).astype(BF16)
    put(gated.at[theirs], r5c, s_5c, r_5c, c, core_e)
    gated[ours] = jnp.dot(expand[ours], scaled, preferred_element_type=F32).astype(BF16)
    landed(r5c, r_5c)
    acc5[...] = (gated[ours].astype(F32) + r5c[...].astype(F32)).astype(BF16)
    hy = h5 // ny
    for d in range(1, ny):
        t = lax.rem(y + d, ny)
        put(acc5.at[pl.ds(al(t * hy, hy), hy)], r5y.at[d - 1], s_5y.at[d - 1], r_5y.at[d - 1], c, exp_at(t, zl, co))
    tot = acc5[pl.ds(al(y * hy, hy), hy)].astype(F32)
    for d in range(1, ny):
        landed(r5y.at[d - 1], r_5y.at[d - 1])
        tot = tot + r5y[d - 1].astype(F32)
    acc6[...] = tot.astype(BF16)
    hz = hy // ZL
    for d in range(1, ZL):
        t = lax.rem(zl + d, ZL)
        put(acc6.at[pl.ds(al(t * hz, hz), hz)], r5z.at[d - 1], s_5z.at[d - 1], r_5z.at[d - 1], c, exp_at(y, t, co))
    tot = acc6[pl.ds(al(zl * hz, hz), hz)].astype(F32)
    for d in range(1, ZL):
        landed(r5z.at[d - 1], r_5z.at[d - 1])
        tot = tot + r5z[d - 1].astype(F32)

    for s in range(nctx):
        snd[s] = tot[s : s + 1]
    for d in range(1, nctx):
        t = lax.rem(c + d, nctx)
        put(snd.at[t], fin.at[c], s_f.at[d - 1], r_f.at[d - 1], t, e)
    fin[c] = snd[c]
    for d in range(1, nctx):
        landed(fin.at[lax.rem(c + nctx - d, nctx)], r_f.at[d - 1])
    out_ref[...] = own[...] + fin[...]
    for copy in sent:
        copy.wait_send()


def local(nctx, nexp, hidden_in, queries, keys, values, out_proj, norm_gain, routes, gates, w_gate, w_up, w_down):
    nx, ny = nctx // ZH, nexp // (ZL * CO)
    tok, hd = queries.shape
    dim = hidden_in.shape[1]
    ffs = w_down.shape[1]
    half = tok // 2
    dy, dz, dc = dim // ny, dim // ny // ZL, dim // nctx
    n_rows, n_out = nctx * SLOTS, nctx * tok
    wide = max(128, tok)
    ring = 4 * (nx // 2) - 2
    V, dma = pltpu.VMEM, pltpu.SemaphoreType.DMA
    pair = lambda n: [dma((n,)), dma((n,))] if n else [dma, dma]
    scratch = [
        V((2, nctx * tok, hd), BF16), V((tok, hd), BF16), V((tok, dim), BF16), V(out_proj.shape, BF16),
        V((1, dim), F32), V(routes.shape, jnp.int32), V(gates.shape, F32),
        V(w_gate.shape[1:], BF16), V(w_up.shape[1:], BF16),
        V((tok, dim), BF16), V((half, dim), BF16), V((half, dim), BF16), V((ny - 1, half, dy), BF16),
        V((half, dy), BF16), V((ZL - 1, half, dz), BF16), V((tok, dim), BF16),
        V((n_rows, wide), F32), V((nctx * ffs, dc), BF16), V((nctx, SLOTS, dim), BF16),
        V((n_rows, 128), F32), V((nctx * ffs, n_rows), BF16), V((n_rows, dc), F32),
        V((n_out, n_rows), BF16), V((n_out, dc), BF16), V((n_out // 2, dc), BF16), V((n_out // 2, dc), BF16),
        V((ny - 1, n_out // 2 // ny, dc), BF16), V((n_out // 2 // ny, dc), BF16), V((ZL - 1, nctx, dc), BF16),
        V((nctx, 1, dc), F32), V((nctx, 1, dc), F32), V((nctx, 1, dc), F32),
        dma((10,)),
        *pair(nctx - 1), *pair(0), *pair(nctx - 1), *pair(nctx - 1),
        *pair(0), *pair(ny - 1), *pair(ZL - 1), *pair(ZL - 1), *pair(ny - 1), *pair(0),
        *pair(0), *pair(ring), *pair(0), *pair(ring),
        *pair(0), *pair(ny - 1), *pair(ZL - 1), *pair(nctx - 1),
    ]
    out = pl.pallas_call(
        functools.partial(kernel, nctx, nexp),
        out_shape=jax.ShapeDtypeStruct((nctx, 1, dc), F32),
        in_specs=[pl.BlockSpec(memory_space=pl.ANY)] * 11,
        out_specs=pl.BlockSpec(memory_space=pltpu.VMEM),
        scratch_shapes=scratch,
        compiler_params=pltpu.CompilerParams(
            collective_id=0, has_side_effects=True, vmem_limit_bytes=40 * 1024 * 1024
        ),
        name="decoder_layer",
    )(hidden_in, queries, keys, values, out_proj, norm_gain.reshape(1, dim), routes, gates, w_gate, w_up, w_down)
    return out.reshape(1, dim).astype(BF16)


def solution(mesh):
    nctx, nexp = mesh.shape["ctx"], mesh.shape["exp"]
    return jax.shard_map(
        functools.partial(local, nctx, nexp),
        mesh=mesh,
        in_specs=(
            P("ctx", None),
            P("ctx", "exp"),
            P("ctx", None),
            P("ctx", None),
            P("exp", None),
            P(),
            P("ctx", None),
            P("ctx", None),
            P("exp", None, "ctx"),
            P("exp", None, "ctx"),
            P("exp", "ctx", None),
        ),
        out_specs=P(("ctx", "exp"), None),
        check_vma=False,
    )
```

time: 1580 us -> 151 us (0.10)
  waiting for transfers between devices: 1450 us -> 0 us
  Pallas kernels: 0 us -> 142 us
  blocking collectives: 95.3 us -> 0 us
    psum x1 -> x0, waiting for transfers between devices: 563 us -> none  [local(): lax.psum(jnp.dot(attended, out_proj, preferred_element_type=jnp.float32),...]
    unnamed x5 -> x0, waiting for transfers between devices: 546 us -> none
    reduce_scatter x1 -> x0, waiting for transfers between devices: 228 us -> none  [local(): lax.psum_scatter(partials.astype(jnp.bfloat16), 'ctx', scatter_dimension=...]
    pallas_call x0 -> x1, Pallas kernels: none -> 142 us  [local(): pl.pallas_call(functools.partial(kernel, nctx, nexp), out_shape=jax.Shape...]
    all_gather x1 -> x0, waiting for transfers between devices: 112 us -> none  [local(): block_rows = lax.all_gather(picked, 'ctx', axis=0, tiled=True)]
    all_gather x2 -> x0, blocking collectives: 95.3 us -> none  [the longest x1 55.5 us: local(): value_piece = lax.all_gather(own_values, 'ctx', axis=0, tiled=True)]
  transfers between devices with their start and end apart: 4 -> 0, of which waited for: 4 -> 0; matrix products, arithmetic and copies ran while one was open for 0% -> 0% of each run, Pallas kernels for 0% -> 0%
where the time goes in v1:
time: 151 us; the launch traced here: 149 us
  Pallas kernels  142 us (94%)
  local copies, waits for them, and re-layouts  6.31 us (4%)
    pallas_call x1, Pallas kernels, local(): pl.pallas_call(functools.partial(kernel, nctx, nexp), out_shape=jax.Shape...  142 us
    unnamed x20, local copies, waits for them, and re-layouts  6.31 us

profile of v1, /device:TPU:1, one launch (start us, length us, event | category | flops | bytes accessed | tf_op | source)
XLA Modules:
  0.0 149.3 jit_solution(14245133803789738952)
XLA Ops:
  0.0 0.0 copy-start.7
  0.0 0.8 copy.12.routes
  0.8 0.0 copy-done.7
  0.8 0.1 copy.13.gates
  0.9 1.6 %copy.14.w_gate = bf16[1,4096,96]{2,1,0:T(8,128)(2,1)S(1)} copy(bf16[1,4096,96]{1,2,0:T(8,128)(2,1)} %param.19) | data formatting | bytes 1572864 | tf_op args[8]
  2.5 0.0 copy-start
  2.5 0.0 copy-start.3
  2.5 0.0 copy-start.4
  2.5 0.0 copy-start.5
  2.5 0.0 copy-start.6
  2.5 1.7 %copy.15.w_up = bf16[1,4096,96]{2,1,0:T(8,128)(2,1)S(1)} copy(bf16[1,4096,96]{1,2,0:T(8,128)(2,1)} %param.20) | data formatting | bytes 1572864 | tf_op args[9]
  4.2 0.0 copy-done
  4.2 0.0 copy-done.3
  4.2 0.0 copy-done.4
  4.2 0.0 copy-done.5
  4.2 0.0 copy-done.6
  4.2 0.0 copy-start.1
  4.2 1.1 copy-done.1
  5.4 0.0 copy-start.2
  5.4 1.0 copy-done.2
  6.4 142.3 %decoder_layer.1 = f32[16,1,256]{2,1,0:T(1,128)S(1)} custom-call(bf16[64,4096]{1,0:T(8,128)(2,1)S(1)} %copy-done.2, bf16[64,128]{1,0:T(8,128)(2,1)S(1)} %copy-done.5, bf16[64,512]{1,0:T(8,128)(2,1)S(1)} %copy-done.3, bf16[64,512]{1,0:T(8,128)(2,1)S(1)} %copy-done.4, bf16[128,4096]{1,0:T(8,128)(2,1)S(1)} %copy-done, f32[1,4096]{1,0:T(1,128)S(1)} %bitcast.2, ...), custom_call_target="tpu_custom_call" | custom-call | tf_op jit(solution)/shard_map/decoder_layer/pallas_call | solution.py:392
  148.7 0.6 convert_element_type.14
Async XLA Ops:
  0.0 0.8 copy-start.7
  2.5 1.7 %copy-start = (bf16[128,4096]{1,0:T(8,128)(2,1)S(1)}, bf16[128,4096]{1,0:T(8,128)(2,1)}, u32[]{:S(2)}) copy-start(bf16[128,4096]{1,0:T(8,128)(2,1)} %out_proj.1) | copy-start | bytes 3145732
  2.5 1.7 %copy-start.3 = (bf16[64,512]{1,0:T(8,128)(2,1)S(1)}, bf16[64,512]{1,0:T(8,128)(2,1)}, u32[]{:S(2)}) copy-start(bf16[64,512]{1,0:T(8,128)(2,1)} %keys.1) | copy-start | bytes 196612
  2.5 1.7 %copy-start.4 = (bf16[64,512]{1,0:T(8,128)(2,1)S(1)}, bf16[64,512]{1,0:T(8,128)(2,1)}, u32[]{:S(2)}) copy-start(bf16[64,512]{1,0:T(8,128)(2,1)} %values.1) | copy-start | bytes 196612
  2.5 1.7 %copy-start.5 = (bf16[64,128]{1,0:T(8,128)(2,1)S(1)}, bf16[64,128]{1,0:T(8,128)(2,1)}, u32[]{:S(2)}) copy-start(bf16[64,128]{1,0:T(8,128)(2,1)} %queries.1) | copy-start | bytes 49156
  2.5 1.7 %copy-start.6 = (f32[4096]{0:T(1024)S(1)}, f32[4096]{0:T(1024)}, u32[]{:S(2)}) copy-start(f32[4096]{0:T(1024)} %param.16) | copy-start | bytes 49156
  4.2 1.1 copy-start.1
  5.4 1.0 copy-start.2

commit v2 on v1

v2 whole, which is shorter than its diff:
```python
import functools

import jax
import jax.numpy as jnp
from jax import lax
from jax.experimental import pallas as pl
from jax.experimental.pallas import tpu as pltpu
from jax.sharding import PartitionSpec as P

HEADS = 64
KVH = 4
SLOTS = 16
ZH, ZL, CO = 2, 4, 2
PARTS = 4
MESH = pl.DeviceIdType.MESH
F32, BF16 = jnp.float32, jnp.bfloat16
NT = (((1,), (1,)), ((), ()))
TN = (((0,), (0,)), ((), ()))


def kernel(
    nctx, nexp,
    hidden_in, queries, keys, values, out_proj, norm_gain, routes, gates, w_gate, w_up, w_down,
    out_ref,
    kv, qv, hid, wo, gain, rt, gt, wgu,
    pbuf, crecv, acc, rsya, rsza, acca, rsyb, rszb, accb, ag,
    mt, wd, rows, act, oacc, expand, gated, r5c, acc5, r5ya, r5za, acc5a, r5yb, r5zb, acc5b, snd, fin, own,
    lsem,
    s_kv, r_kv, s_kvc, r_kvc, s_sel, r_sel, s_wd, r_wd,
    s_c, r_c, s_ya, r_ya, s_za, r_za, s_yb, r_yb, s_zb, r_zb,
    s_gya, r_gya, s_gza, r_gza, s_gyb, r_gyb, s_gzb, r_gzb, s_gc, r_gc,
    s_zh, r_zh, s_ring, r_ring, s_azh, r_azh, s_aring, r_aring,
    s_5c, r_5c, s_5ya, r_5ya, s_5za, r_5za, s_5yb, r_5yb, s_5zb, r_5zb, s_f, r_f,
):
    nx, ny = nctx // ZH, nexp // (ZL * CO)
    tok, hd = qv.shape
    dim = hid.shape[1]
    ffs = w_down.shape[1]
    half = tok // 2
    quarter = half // 2
    dp = dim // ny // ZL
    dc = dim // nctx
    lanes = act.shape[1] // nctx
    up_at = wgu.shape[0] // 2
    c, e = lax.axis_index("ctx"), lax.axis_index("exp")
    x, zh = lax.div(c, ZH), lax.rem(c, ZH)
    y, zl, co = lax.div(e, ZL * CO), lax.rem(lax.div(e, CO), ZL), lax.rem(e, CO)
    core_e = e + 1 - 2 * co
    oco = 1 - co

    def ctx_at(xx, hh):
        return lax.rem(xx + nx, nx) * ZH + hh

    def exp_at(yy, zz, cc):
        return (yy * ZL + zz) * CO + cc

    sent = []

    def put(src, dst, ssem, rsem, cc, ee):
        copy = pltpu.make_async_remote_copy(
            src_ref=src, dst_ref=dst, send_sem=ssem, recv_sem=rsem,
            device_id=(cc, ee), device_id_type=MESH,
        )
        copy.start()
        sent.append(copy)
        return copy

    def landed(ref, rsem):
        pltpu.make_async_remote_copy(
            src_ref=ref, dst_ref=ref, send_sem=rsem, recv_sem=rsem,
            device_id=(c, core_e), device_id_type=MESH,
        ).wait_recv()

    def al(v, m):
        return pl.multiple_of(v, m)

    def seg(i, n):
        return pl.ds(al(i * n, n), n)

    group = HEADS // KVH
    heads_here = max(1, HEADS // nexp)
    kv_col = al(lax.div(e * heads_here, group) * hd, hd)
    own_kv = kv.at[co, pl.ds(al(c * tok, tok), tok)]

    @pl.when(co == 0)
    def _():
        pltpu.make_async_copy(keys.at[:, pl.ds(kv_col, hd)], own_kv, lsem.at[0]).start()

    @pl.when(co == 1)
    def _():
        pltpu.make_async_copy(values.at[:, pl.ds(kv_col, hd)], own_kv, lsem.at[0]).start()

    own_wd = pltpu.make_async_copy(
        w_down.at[0, :, pl.ds(al(c * dc, dc), dc)], wd.at[c, :ffs], lsem.at[1]
    )
    loads = [
        pltpu.make_async_copy(src, dst, lsem.at[2 + i])
        for i, (src, dst) in enumerate([
            (routes, rt), (gates, gt), (queries, qv), (out_proj, wo), (hidden_in, hid),
            (norm_gain, gain), (w_gate.at[0], wgu.at[:ffs]), (w_up.at[0], wgu.at[pl.ds(up_at, ffs)]),
        ])
    ]
    for load in loads:
        load.start()
    own_wd.start()

    barrier = pltpu.get_barrier_semaphore()

    def greet(cc, ee):
        pl.semaphore_signal(barrier, inc=1, device_id=(cc, ee), device_id_type=MESH)

    for d in range(1, nctx):
        greet(lax.rem(c + d, nctx), e)
    for d in range(1, ny):
        greet(c, exp_at(lax.rem(y + d, ny), zl, co))
    for d in range(1, ZL):
        greet(c, exp_at(y, lax.rem(zl + d, ZL), co))
    greet(c, core_e)
    pl.semaphore_wait(barrier, (nctx - 1) + (ny - 1) + (ZL - 1) + 1)

    pltpu.make_async_copy(keys.at[:, pl.ds(kv_col, hd)], own_kv, lsem.at[0]).wait()
    def kv_at(block):
        return kv.at[co, pl.ds(al(block * tok, tok), tok)]

    partner = ctx_at(x, 1 - zh)
    for d in range(1, nctx):
        put(own_kv, own_kv, s_kv.at[d - 1], r_kv.at[d - 1], lax.rem(c + d, nctx), e)
    waiting = list(range(1, nctx))

    def some_down(count):
        for d in waiting[:count]:
            t = lax.rem(c + d, nctx)
            put(w_down.at[0, :, seg(t, dc)], wd.at[c, :ffs], s_wd.at[d - 1], r_wd.at[d - 1], t, e)
        del waiting[:count]

    some_down(15)

    if up_at > ffs:
        wgu[ffs:up_at] = jnp.zeros((up_at - ffs, dim), BF16)
        wgu[up_at + ffs :] = jnp.zeros((up_at - ffs, dim), BF16)
        wd[:, ffs:, :] = jnp.zeros((nctx, lanes - ffs, dc), BF16)

    loads[0].wait()
    loads[1].wait()
    hit = rt[...] == e
    member_r = jnp.max(jnp.where(hit, 1.0, 0.0), axis=0, keepdims=True)
    weight_r = jnp.sum(jnp.where(hit, gt[...], 0.0), axis=0, keepdims=True)
    wide = mt.shape[1]
    t_row = lax.broadcasted_iota(jnp.int32, (tok, tok), 0)
    t_col = lax.broadcasted_iota(jnp.int32, (tok, tok), 1)
    member = jnp.sum(jnp.where(t_row == t_col, member_r, 0.0), axis=1, keepdims=True)
    count_r = jnp.sum(jnp.where(t_row <= t_col, member, 0.0), axis=0, keepdims=True)
    if wide > tok:
        blank = jnp.zeros((1, wide - tok), F32)
        member_r = jnp.concatenate([member_r, blank], axis=1)
        weight_r = jnp.concatenate([weight_r, blank], axis=1)
        count_r = jnp.concatenate([count_r, blank], axis=1)
    slot_i = lax.broadcasted_iota(jnp.int32, (SLOTS, wide), 0).astype(F32)
    chosen = (count_r - 1.0 == slot_i) & (member_r > 0.0)
    own_mt = mt.at[pl.ds(al(c * SLOTS, SLOTS), SLOTS)]
    own_mt[...] = jnp.where(chosen, weight_r, 0.0).astype(BF16)
    pick = jnp.where(chosen, 1.0, 0.0)
    mine = jnp.where(lax.broadcasted_iota(jnp.int32, (SLOTS, wide), 1) == e, 1.0, 0.0)
    pick2 = jnp.concatenate([pick, mine], axis=0)[:, :tok].astype(BF16)

    for d in range(1, nctx):
        put(own_mt, own_mt, s_sel.at[d - 1], r_sel.at[d - 1], lax.rem(c + d, nctx), e)
    for d in range(1, nctx):
        landed(kv_at(lax.rem(c + nctx - d, nctx)), r_kv.at[d - 1])
    put(kv.at[co], kv.at[co], s_kvc, r_kvc, c, core_e)
    some_down(0)
    loads[2].wait()
    landed(kv.at[oco], r_kvc)

    scores = lax.dot_general(qv[...], kv[0], NT, preferred_element_type=F32) * hd ** (-0.5)
    n_keys = kv.shape[1]
    q_pos = c * tok + lax.broadcasted_iota(jnp.int32, (tok, n_keys), 0)
    visible = lax.broadcasted_iota(jnp.int32, (tok, n_keys), 1) <= q_pos
    masked = jnp.where(visible, scores, -1e30)
    prob = jnp.where(visible, jnp.exp(masked - jnp.max(masked, axis=1, keepdims=True)), 0.0)
    total = jnp.sum(prob, axis=1, keepdims=True)
    numer = jnp.dot(prob.astype(BF16), kv[1], preferred_element_type=F32)
    att = (numer / total).astype(BF16)
    loads[3].wait()
    n_col = 8
    dw = dim // n_col
    for j in range(n_col):
        cols = pl.ds(j * dw, dw)
        pbuf[:, cols] = jnp.dot(att, wo[:, cols], preferred_element_type=F32).astype(BF16)

    def across_y(d):
        return lax.rem(y + d, ny)

    def across_z(d):
        return lax.rem(zl + d, ZL)

    n_out = tok * nctx

    def place(i, _):
        blk = n_out // 8
        r = i * blk + lax.broadcasted_iota(jnp.int32, (blk, wide), 0)
        t = lax.broadcasted_iota(jnp.int32, (blk, wide), 1)
        p = lax.div(r, nctx)
        token = lax.rem(p, tok // CO) * CO + lax.div(p, tok // CO)
        pattern = jnp.where(t == token, 1.0, 0.0).astype(BF16)
        taken = jnp.where(mt[...].astype(F32) > 0.0, 1.0, 0.0).astype(BF16)
        hits = lax.dot_general(pattern, taken, NT, preferred_element_type=F32)
        r = i * blk + lax.broadcasted_iota(jnp.int32, hits.shape, 0)
        s = lax.broadcasted_iota(jnp.int32, hits.shape, 1)
        keep = lax.rem(r, nctx) == lax.div(s, SLOTS)
        expand[pl.ds(al(i * blk, blk), blk), :] = jnp.where(keep, hits, 0.0).astype(BF16)
        return 0

    def place_all():
        for d in range(1, nctx):
            landed(mt.at[seg(lax.rem(c + nctx - d, nctx), SLOTS)], r_sel.at[d - 1])
        lax.fori_loop(0, 8, place, 0)

    put(pbuf.at[pl.ds(al(oco * half, half), half)], crecv, s_c, r_c, c, core_e)
    some_down(0)
    landed(crecv, r_c)
    mine_rows = pl.ds(al(co * half, half), half)
    for j in range(n_col):
        cols = pl.ds(j * dw, dw)
        acc[:, cols] = (pbuf[mine_rows, cols].astype(F32) + crecv[:, cols].astype(F32)).astype(BF16)
    top, low = pl.ds(0, quarter), pl.ds(quarter, quarter)
    dya, dzb = dp * ZL, dp * ny

    for d in range(1, ny):
        t = across_y(d)
        put(acc.at[top, seg(t, dya)], rsya.at[d - 1], s_ya.at[d - 1], r_ya.at[d - 1], c, exp_at(t, zl, co))
    for d in range(1, ZL):
        t = across_z(d)
        put(acc.at[low, seg(t, dzb)], rszb.at[d - 1], s_zb.at[d - 1], r_zb.at[d - 1], c, exp_at(y, t, co))
    some_down(nctx)
    place_all()
    tot = acc[low, seg(zl, dzb)].astype(F32)
    for d in range(1, ZL):
        landed(rszb.at[d - 1], r_zb.at[d - 1])
        tot = tot + rszb[d - 1].astype(F32)
    accb[...] = tot.astype(BF16)
    for d in range(1, ny):
        t = across_y(d)
        put(accb.at[:, seg(t, dp)], rsyb.at[d - 1], s_yb.at[d - 1], r_yb.at[d - 1], c, exp_at(t, zl, co))
    tot = acc[top, seg(y, dya)].astype(F32)
    for d in range(1, ny):
        landed(rsya.at[d - 1], r_ya.at[d - 1])
        tot = tot + rsya[d - 1].astype(F32)
    acca[...] = tot.astype(BF16)
    for d in range(1, ZL):
        t = across_z(d)
        put(acca.at[:, seg(t, dp)], rsza.at[d - 1], s_za.at[d - 1], r_za.at[d - 1], c, exp_at(y, t, co))
    ag_top = pl.ds(al(co * half, quarter), quarter)
    ag_low = pl.ds(al(co * half + quarter, quarter), quarter)

    def cell(rows_at, at, n):
        return ag.at[rows_at, pl.ds(al(at, n), n)]

    tot = accb[:, seg(y, dp)].astype(F32)
    for d in range(1, ny):
        landed(rsyb.at[d - 1], r_yb.at[d - 1])
        tot = tot + rsyb[d - 1].astype(F32)
    own_b = cell(ag_low, zl * dzb + y * dp, dp)
    own_b[...] = tot.astype(BF16)
    for d in range(1, ny):
        put(own_b, own_b, s_gyb.at[d - 1], r_gyb.at[d - 1], c, exp_at(across_y(d), zl, co))
    tot = acca[:, seg(zl, dp)].astype(F32)
    for d in range(1, ZL):
        landed(rsza.at[d - 1], r_za.at[d - 1])
        tot = tot + rsza[d - 1].astype(F32)
    own_a = cell(ag_top, y * dya + zl * dp, dp)
    own_a[...] = tot.astype(BF16)
    for d in range(1, ZL):
        put(own_a, own_a, s_gza.at[d - 1], r_gza.at[d - 1], c, exp_at(y, across_z(d), co))
    for d in range(1, ZL):
        landed(cell(ag_top, y * dya + across_z(ZL - d) * dp, dp), r_gza.at[d - 1])
    line = cell(ag_top, y * dya, dya)
    for d in range(1, ny):
        put(line, line, s_gya.at[d - 1], r_gya.at[d - 1], c, exp_at(across_y(d), zl, co))
    for d in range(1, ny):
        landed(cell(ag_low, zl * dzb + across_y(ny - d) * dp, dp), r_gyb.at[d - 1])
    line = cell(ag_low, zl * dzb, dzb)
    for d in range(1, ZL):
        put(line, line, s_gzb.at[d - 1], r_gzb.at[d - 1], c, exp_at(y, across_z(d), co))
    for d in range(1, ZL):
        landed(cell(ag_low, across_z(ZL - d) * dzb, dzb), r_gzb.at[d - 1])
    for d in range(1, ny):
        landed(cell(ag_top, across_y(ny - d) * dya, dya), r_gya.at[d - 1])
    put(ag.at[mine_rows], ag.at[mine_rows], s_gc, r_gc, c, core_e)
    loads[4].wait()
    loads[5].wait()
    landed(ag.at[pl.ds(al(oco * half, half), half)], r_gc)

    square = jnp.zeros((SLOTS, 1), F32)
    mixes = []
    for j in range(n_col):
        cols = pl.ds(j * dw, dw)
        mixed = jnp.dot(pick2, ag[:, cols], preferred_element_type=F32) + jnp.dot(
            pick2, hid[:, cols], preferred_element_type=F32
        )
        square = square + jnp.sum(mixed[:SLOTS] * mixed[:SLOTS], axis=1, keepdims=True)
        own_part = mixed[SLOTS : SLOTS + 1]
        for k in range(max(1, dw // dc)):
            if dw >= dc:
                own[j * (dw // dc) + k] = own_part[:, k * dc : (k + 1) * dc]
            else:
                own[j * dw // dc, :, (j * dw) % dc : (j * dw) % dc + dw] = own_part
        mixes.append(mixed[:SLOTS])
    scale = lax.rsqrt(square / dim + 1e-06)
    for j in range(n_col):
        cols = pl.ds(j * dw, dw)
        rows[c, :, cols] = (mixes[j] * scale * gain[:, cols]).astype(BF16)

    far = nx // 2

    def route(parts, lag):
        hops, first, n = {}, {}, 0
        for kind in (0, 1):
            for h in range(parts):
                for step in (1, -1):
                    key = (step, kind, h)
                    most = far - 1 if lag and kind else far
                    hops[key] = far if (step == 1) == (h % 2 == 0) and most == far else far - 1
                    first[key] = n
                    n += hops[key]
        return hops, first

    side = (zh, 1 - zh)

    def ring_send(at, s_ring, r_ring, hops, first):
        def send(key, k):
            step, kind, h = key
            if k < hops[key]:
                ref = at(ctx_at(x - step * k, side[kind]), h)
                i = first[key] + k
                put(ref, ref, s_ring.at[i], r_ring.at[i], ctx_at(x + step, zh), e)

        return send

    def ring(at, parts, s_zh, r_zh, s_ring, r_ring, meanwhile, use, lag):
        hops, first = route(parts, lag)
        send = ring_send(at, s_ring, r_ring, hops, first)

        def wait(key, k):
            step, kind, h = key
            landed(at(ctx_at(x - step * k, side[kind]), h), r_ring.at[first[key] + k - 1])

        for h in range(parts):
            if lag:
                put(at(c, h), at(c, h), s_zh.at[h], r_zh.at[h], partner, e)
            for step in (1, -1):
                send((step, 0, h), 0)
        meanwhile()
        for k in range(1, far + 1 + lag):
            for h in range(parts):
                for step in (1, -1):
                    if k <= hops[(step, 0, h)]:
                        wait((step, 0, h), k)
                        send((step, 0, h), k)
                        if lag and k == far:
                            across = at(ctx_at(x - far, zh), h)
                            put(across, across, s_zh.at[parts + h], r_zh.at[parts + h], partner, e)
            m = k - lag
            for h in range(parts):
                if m == 0:
                    landed(at(partner, h), r_zh.at[h])
                if lag and m == far:
                    landed(at(ctx_at(x - far, 1 - zh), h), r_zh.at[parts + h])
                for step in (1, -1):
                    if 0 < m <= hops[(step, 1, h)]:
                        wait((step, 1, h), m)
                    if 0 <= m <= hops[(step, 1, h)]:
                        send((step, 1, h), m)
            use(k, m)

    def places(k):
        return [k] if k in (0, far) else [k, -k]

    def meanwhile():
        for load in loads[6:]:
            load.wait()

    kc = dim // 4

    def expert(k, m):
        spots = [lax.rem(x - i + nx, nx) for i in places(m)]
        blocks = [spot * ZH + h for spot in spots for h in range(ZH)]
        gu = jnp.zeros((len(blocks) * SLOTS, 2 * up_at), F32)
        for k in range(4):
            part = pl.ds(k * kc, kc)
            rows_in = jnp.concatenate([rows[b, :, part] for b in blocks], axis=0)
            gu = gu + lax.dot_general(rows_in, wgu[:, part], NT, preferred_element_type=F32)
        g, u = gu[:, :up_at], gu[:, up_at:]
        a = (g / (1.0 + jnp.exp(-g)) * u).astype(BF16)
        for i, b in enumerate(blocks):
            act[seg(b, SLOTS), seg(c, lanes)] = a[i * SLOTS : (i + 1) * SLOTS]
        for i, spot in zip(places(m), spots):
            piece = act.at[seg(spot, ZH * SLOTS), seg(c, lanes)]
            put(piece, piece, s_azh.at[i % nx], r_azh.at[i % nx], partner, e)

    dpart = dim // PARTS
    ring(
        lambda b, h: rows.at[b, :, pl.ds(h * dpart, dpart)],
        PARTS, s_zh, r_zh, s_ring, r_ring, meanwhile, expert, 1,
    )

    def add(blocks):
        tot = oacc[...]
        for b in blocks:
            tot = tot + jnp.dot(act[:, seg(b, lanes)], wd[b], preferred_element_type=F32)
        oacc[...] = tot

    n_half = nctx * SLOTS // 2

    earlier = list(sent)
    sent.clear()

    def from_partner():
        for i in range(nx):
            landed(act.at[seg(lax.rem(x + i, nx), ZH * SLOTS), seg(partner, lanes)], r_azh.at[(nx - i) % nx])
        for h in (0, 1):
            for step in (1, -1):
                relay((step, 1, h), 0)
        own_wd.wait()
        for d in range(1, nctx):
            landed(wd.at[lax.rem(c + nctx - d, nctx), :ffs], r_wd.at[d - 1])
        oacc[...] = jnp.zeros_like(oacc)
        add([c, partner])
        for copy in earlier:
            copy.wait_send()

    def down(k, m):
        add([ctx_at(x - i, h) for i in places(k) for h in range(ZH)])

    def act_at(b, h):
        return act.at[pl.ds(h * n_half, n_half), seg(b, lanes)]

    relay = ring_send(act_at, s_aring, r_aring, *route(2, 0))
    ring(act_at, 2, None, None, s_aring, r_aring, from_partner, down, 0)

    scaled = (oacc[...] * jnp.sum(mt[...].astype(F32), axis=1, keepdims=True)).astype(BF16)
    h5 = n_out // 2
    blocks5 = (ny, ZL, nctx, dc)

    def spread(side):
        return jnp.dot(expand[seg(side, h5)], scaled, preferred_element_type=F32).astype(BF16).reshape(blocks5)

    gated[oco] = spread(oco)
    put(gated.at[oco], r5c, s_5c, r_5c, c, core_e)
    gated[co] = spread(co)
    landed(r5c, r_5c)
    acc5[...] = (gated[co].astype(F32) + r5c[...].astype(F32)).astype(BF16)
    hc = dc // 2
    left, right = pl.ds(0, hc), pl.ds(hc, hc)
    for d in range(1, ny):
        t = across_y(d)
        put(acc5.at[t, :, :, left], r5ya.at[d - 1], s_5ya.at[d - 1], r_5ya.at[d - 1], c, exp_at(t, zl, co))
    for d in range(1, ZL):
        t = across_z(d)
        put(acc5.at[:, t, :, right], r5zb.at[d - 1], s_5zb.at[d - 1], r_5zb.at[d - 1], c, exp_at(y, t, co))
    tot = acc5[:, zl, :, right].astype(F32)
    for d in range(1, ZL):
        landed(r5zb.at[d - 1], r_5zb.at[d - 1])
        tot = tot + r5zb[d - 1].astype(F32)
    acc5b[...] = tot.astype(BF16)
    for d in range(1, ny):
        t = across_y(d)
        put(acc5b.at[t], r5yb.at[d - 1], s_5yb.at[d - 1], r_5yb.at[d - 1], c, exp_at(t, zl, co))
    tot = acc5[y, :, :, left].astype(F32)
    for d in range(1, ny):
        landed(r5ya.at[d - 1], r_5ya.at[d - 1])
        tot = tot + r5ya[d - 1].astype(F32)
    acc5a[...] = tot.astype(BF16)
    for d in range(1, ZL):
        t = across_z(d)
        put(acc5a.at[t], r5za.at[d - 1], s_5za.at[d - 1], r_5za.at[d - 1], c, exp_at(y, t, co))
    tot_b = acc5b[y].astype(F32)
    for d in range(1, ny):
        landed(r5yb.at[d - 1], r_5yb.at[d - 1])
        tot_b = tot_b + r5yb[d - 1].astype(F32)
    tot_a = acc5a[zl].astype(F32)
    for d in range(1, ZL):
        landed(r5za.at[d - 1], r_5za.at[d - 1])
        tot_a = tot_a + r5za[d - 1].astype(F32)
    tot = jnp.concatenate([tot_a, tot_b], axis=1)

    for s in range(nctx):
        snd[s] = tot[s : s + 1]
    for d in range(1, nctx):
        t = lax.rem(c + d, nctx)
        put(snd.at[t], fin.at[c], s_f.at[d - 1], r_f.at[d - 1], t, e)
    fin[c] = snd[c]
    for d in range(1, nctx):
        landed(fin.at[lax.rem(c + nctx - d, nctx)], r_f.at[d - 1])
    out_ref[...] = own[...] + fin[...]
    for copy in sent:
        copy.wait_send()


def local(nctx, nexp, hidden_in, queries, keys, values, out_proj, norm_gain, routes, gates, w_gate, w_up, w_down):
    nx, ny = nctx // ZH, nexp // (ZL * CO)
    tok, hd = queries.shape
    dim = hidden_in.shape[1]
    ffs = w_down.shape[1]
    half = tok // 2
    quarter = half // 2
    dp, dc = dim // ny // ZL, dim // nctx
    n_rows, n_out = nctx * SLOTS, nctx * tok
    wide = max(128, tok)
    lanes = -(-ffs // 128) * 128
    V, dma = pltpu.VMEM, pltpu.SemaphoreType.DMA
    pair = lambda n: [dma((n,)), dma((n,))] if n else [dma, dma]
    scratch = [
        V((2, nctx * tok, hd), BF16), V((tok, hd), BF16), V((tok, dim), BF16), V(out_proj.shape, BF16),
        V((1, dim), F32), V(routes.shape[::-1], jnp.int32), V(gates.shape[::-1], F32), V((2 * lanes, dim), BF16),
        V((tok, dim), BF16), V((half, dim), BF16), V((half, dim), BF16),
        V((ny - 1, quarter, dp * ZL), BF16), V((ZL - 1, quarter, dp), BF16), V((quarter, dp * ZL), BF16),
        V((ny - 1, quarter, dp), BF16), V((ZL - 1, quarter, dp * ny), BF16), V((quarter, dp * ny), BF16),
        V((tok, dim), BF16),
        V((n_rows, wide), BF16), V((nctx, lanes, dc), BF16), V((nctx, SLOTS, dim), BF16),
        V((n_rows, nctx * lanes), BF16), V((n_rows, dc), F32),
        V((n_out, n_rows), BF16), V((CO, ny, ZL, nctx, dc), BF16), V((ny, ZL, nctx, dc), BF16), V((ny, ZL, nctx, dc), BF16),
        V((ny - 1, ZL, nctx, dc // 2), BF16), V((ZL - 1, nctx, dc // 2), BF16), V((ZL, nctx, dc // 2), BF16),
        V((ny - 1, nctx, dc // 2), BF16), V((ZL - 1, ny, nctx, dc // 2), BF16), V((ny, nctx, dc // 2), BF16),
        V((nctx, 1, dc), F32), V((nctx, 1, dc), F32), V((nctx, 1, dc), F32),
        dma((10,)),
        *pair(nctx - 1), *pair(0), *pair(nctx - 1), *pair(nctx - 1),
        *pair(0), *pair(ny - 1), *pair(ZL - 1), *pair(ny - 1), *pair(ZL - 1),
        *pair(ny - 1), *pair(ZL - 1), *pair(ny - 1), *pair(ZL - 1), *pair(0),
        *pair(2 * PARTS), *pair(PARTS * (4 * (nx // 2) - 3)), *pair(nx), *pair(8 * (nx // 2) - 4),
        *pair(0), *pair(ny - 1), *pair(ZL - 1), *pair(ny - 1), *pair(ZL - 1), *pair(nctx - 1),
    ]
    out = pl.pallas_call(
        functools.partial(kernel, nctx, nexp),
        out_shape=jax.ShapeDtypeStruct((nctx, 1, dc), F32),
        in_specs=[pl.BlockSpec(memory_space=pl.ANY)] * 11,
        out_specs=pl.BlockSpec(memory_space=pltpu.VMEM),
        scratch_shapes=scratch,
        compiler_params=pltpu.CompilerParams(
            collective_id=0, has_side_effects=True, vmem_limit_bytes=60 * 1024 * 1024
        ),
        name="decoder_layer",
    )(
        hidden_in, queries, keys, values, out_proj, norm_gain.reshape(1, dim), routes.T, gates.T,
        jnp.swapaxes(w_gate, 1, 2), jnp.swapaxes(w_up, 1, 2), w_down,
    )
    return out.reshape(1, dim).astype(BF16)


def solution(mesh):
    nctx, nexp = mesh.shape["ctx"], mesh.shape["exp"]
    return jax.shard_map(
        functools.partial(local, nctx, nexp),
        mesh=mesh,
        in_specs=(
            P("ctx", None),
            P("ctx", "exp"),
            P("ctx", None),
            P("ctx", None),
            P("exp", None),
            P(),
            P("ctx", None),
            P("ctx", None),
            P("exp", None, "ctx"),
            P("exp", None, "ctx"),
            P("exp", "ctx", None),
        ),
        out_specs=P(("ctx", "exp"), None),
        check_vma=False,
    )
```

time: 151 us -> 142 us (0.940)
  local copies, waits for them, and re-layouts: 6.31 us -> 0 us
  Pallas kernels: 142 us -> 140 us
    unnamed x20 -> x0, local copies, waits for them, and re-layouts: 6.31 us -> none
    pallas_call x1, Pallas kernels: 142 us -> 140 us  [local(): pl.pallas_call(functools.partial(kernel, nctx, nexp), out_shape=jax.Shape...]
where the time goes in v2:
time: 142 us; the launch traced here: 141 us
  Pallas kernels  140 us (99%)
    pallas_call x1, Pallas kernels, local(): pl.pallas_call(functools.partial(kernel, nctx, nexp), out_shape=jax.Shape...  140 us

profile of v2, /device:TPU:1, one launch (start us, length us, event | category | flops | bytes accessed | tf_op | source)
XLA Modules:
  0.0 141.5 jit_solution(13257281604254733414)
XLA Ops:
  0.0 140.1 %decoder_layer.1 = f32[16,1,256]{2,1,0:T(1,128)} custom-call(bf16[64,4096]{1,0:T(8,128)(2,1)} %hidden_in.1, bf16[64,128]{1,0:T(8,128)(2,1)} %queries.1, bf16[64,512]{1,0:T(8,128)(2,1)} %keys.1, bf16[64,512]{1,0:T(8,128)(2,1)} %values.1, bf16[128,4096]{1,0:T(8,128)(2,1)} %out_proj.1, f32[1,4096]{1,0:T(1,128)} %bitcast.8, s32[8,64]{1,0:T(8,128)} %bitcast.9, ...), custom_call_target="tpu_custom_call" | custom-call | tf_op jit(solution)/shard_map/decoder_layer/pallas_call | solution.py:533
  140.1 1.3 convert_element_type.14

commit v3 on v2

--- a/solution.py
+++ b/solution.py
@@ -133,7 +133,6 @@
             put(w_down.at[0, :, seg(t, dc)], wd.at[c, :ffs], s_wd.at[d - 1], r_wd.at[d - 1], t, e)
         del waiting[:count]
 
-    some_down(15)
 
     if up_at > ffs:
         wgu[ffs:up_at] = jnp.zeros((up_at - ffs, dim), BF16)
@@ -165,10 +164,11 @@
 
     for d in range(1, nctx):
         put(own_mt, own_mt, s_sel.at[d - 1], r_sel.at[d - 1], lax.rem(c + d, nctx), e)
+    some_down(8)
     for d in range(1, nctx):
         landed(kv_at(lax.rem(c + nctx - d, nctx)), r_kv.at[d - 1])
     put(kv.at[co], kv.at[co], s_kvc, r_kvc, c, core_e)
-    some_down(0)
+    some_down(4)
     loads[2].wait()
     landed(kv.at[oco], r_kvc)
 
@@ -217,7 +217,7 @@
         lax.fori_loop(0, 8, place, 0)
 
     put(pbuf.at[pl.ds(al(oco * half, half), half)], crecv, s_c, r_c, c, core_e)
-    some_down(0)
+    some_down(3)
     landed(crecv, r_c)
     mine_rows = pl.ds(al(co * half, half), half)
     for j in range(n_col):

time: 142 us -> 142 us (level)
  no operation moved by 1% of the time
where the time goes in v3:
time: 142 us
  Pallas kernels  140 us (99%)
    pallas_call x1, Pallas kernels, local(): pl.pallas_call(functools.partial(kernel, nctx, nexp), out_shape=jax.Shape...  140 us

profile of v3, /device:TPU:1, one launch (start us, length us, event | category | flops | bytes accessed | tf_op | source)
XLA Modules:
  0.0 141.8 jit_solution(17770173025007148894)
XLA Ops:
  0.0 140.4 %decoder_layer.1 = f32[16,1,256]{2,1,0:T(1,128)} custom-call(bf16[64,4096]{1,0:T(8,128)(2,1)} %hidden_in.1, bf16[64,128]{1,0:T(8,128)(2,1)} %queries.1, bf16[64,512]{1,0:T(8,128)(2,1)} %keys.1, bf16[64,512]{1,0:T(8,128)(2,1)} %values.1, bf16[128,4096]{1,0:T(8,128)(2,1)} %out_proj.1, f32[1,4096]{1,0:T(1,128)} %bitcast.8, s32[8,64]{1,0:T(8,128)} %bitcast.9, ...), custom_call_target="tpu_custom_call" | custom-call | tf_op jit(solution)/shard_map/decoder_layer/pallas_call | solution.py:533
  140.5 1.3 convert_element_type.14
